TPU v7x, 512 devices: a whole 4x8x8 slice. The times are simulated.
512 devices in a mesh: ctx: 16 (over x, y_hi, core), tp: 32 (over y_lo, z).
Axes of the slice: x: 4, y: 8 (y_hi: 2, y_lo: 4; y = y_hi * 4 + y_lo), z: 8, core: 2. Of those that a mesh axis runs over, the one named last changes fastest.
Arguments:
- tokens: bfloat16 [8192, 8192], P('ctx', 'tp'), may hold values from -400 to 400
- norm_gain: bfloat16 [8192], P('tp'), may hold values from 0.099609375 to 1.8984375
- in_weight: bfloat16 [8192, 3, 8192], P('ctx', None, 'tp'), may hold values from -0.0625 to 0.0625
- short_weight: float32 [3, 3, 8192], P(None, None, 'tp'), may hold values from -3.5 to 3.5
- filters: bfloat16 [512, 128], P('tp'), may hold values from -0.5 to 0.5
Outputs:
- mixed: bfloat16 [8192, 8192], P('ctx', 'tp')
All inputs are finite; a program needn't handle non-finite values.
Results may differ from a plain program's by a relative error of at most 0.0091.
Values may be sent and summed in bfloat16 or wider, within the bound.
A program may use at most 128 MiB of HBM per device.

v0:
```python
import jax
import jax.numpy as jnp
from jax import lax
from jax.sharding import PartitionSpec as P


def from_behind(block, axis, distance):
    devices = range(lax.axis_size(axis))
    route = [(i - distance, i) for i in devices if i - distance in devices]
    return lax.ppermute(block, axis, route)


def toeplitz_pair(rows, taps):
    above = jnp.arange(taps)[:, None]
    across = jnp.arange(taps)[None, :]
    index = (across - above) % taps
    full = rows[:, index]
    zero = jnp.zeros((), rows.dtype)
    return (jnp.where(across >= above, full, zero), jnp.where(across < above, full, zero))


def filter_blocks(stack, before, rows):
    near, far = toeplitz_pair(rows, stack.shape[3])
    total = jnp.einsum("gcbs,gsi->gcbi", stack, near, preferred_element_type=jnp.float32)
    return total + jnp.einsum("gcbs,gsi->gcbi", before, far, preferred_element_type=jnp.float32)


def per_device(tokens, norm_gain, in_weight, short_weight, filters):
    count, local_width = tokens.shape
    xlocal = tokens.astype(jnp.float32)
    partial_sq = jnp.sum(xlocal * xlocal, axis=1)
    total_sq = lax.psum(partial_sq, "tp")
    scale = lax.rsqrt(total_sq / (local_width * lax.axis_size("tp")) + 1e-06)
    normed_local = (xlocal * scale[:, None] * norm_gain.astype(jnp.float32)).astype(jnp.bfloat16)
    whole = lax.all_gather(normed_local, "tp", axis=1, tiled=True)
    piece = lax.all_gather(in_weight, "ctx", axis=0, tiled=True)
    depth = piece.shape[0]
    projected = jnp.dot(
        whole, piece.reshape(depth, 3 * local_width), preferred_element_type=jnp.float32
    )
    proj = projected.reshape(count, 3, local_width).astype(jnp.bfloat16)
    short_taps = short_weight.shape[0]
    earlier = from_behind(proj[count - (short_taps - 1) :], "ctx", 1)
    extended = jnp.concatenate([earlier, proj], 0).astype(jnp.float32)
    feat = jnp.zeros((count, 3, local_width), jnp.float32)
    for tap in range(short_taps):
        feat = (
            feat + short_weight[tap] * extended[short_taps - 1 - tap : short_taps - 1 - tap + count]
        )
    gated = (feat[:, 1] * feat[:, 2]).astype(jnp.bfloat16)
    taps = filters.shape[1]
    members = local_width // filters.shape[0]
    channel_major = gated.T
    regrouped = lax.all_to_all(channel_major, "ctx", split_axis=0, concat_axis=1, tiled=True)
    channels, length = regrouped.shape
    groups = channels // members
    stack = regrouped.reshape(groups, members, length // taps, taps)
    before = jnp.concatenate(
        [jnp.zeros((groups, members, 1, taps), jnp.bfloat16), stack[:, :, :-1]], 2
    )
    rows = lax.dynamic_slice_in_dim(filters, lax.axis_index("ctx") * groups, groups, 0)
    filtered = filter_blocks(stack, before, rows).reshape(channels, length).astype(jnp.bfloat16)
    returned = lax.all_to_all(filtered, "ctx", split_axis=1, concat_axis=0, tiled=True)
    conv = returned.T
    return (feat[:, 0] * conv.astype(jnp.float32)).astype(jnp.bfloat16)


def solution(mesh):
    placed = (P("ctx", "tp"), P("tp"), P("ctx", None, "tp"), P(None, None, "tp"), P("tp", None))
    return jax.shard_map(
        per_device, mesh=mesh, in_specs=placed, out_specs=P("ctx", "tp"), check_vma=False
    )
```

profile of v0, /device:TPU:1, one launch (start us, length us, event | category | flops | bytes accessed | tf_op | source)
XLA Modules:
  0.0 574.4 jit_solution(13637236991096005759)
XLA Ops:
  6.5 1.2 fusion.11
  7.7 73.2 %psum.7 = f32[512]{0:T(512)S(1)} all-reduce(f32[512]{0:T(512)S(1)} %fusion.11), channel_id=1, replica_groups=mesh['ctx'=16,'tp'=32] {'tp'}, use_global_device_ids=true, to_apply=%region_1.0 | all-reduce | flops 512 | bytes 4096 | tf_op jit(solution)/shard_map/psum | solution.py:32
  80.9 0.7 convert_element_type.44
  81.6 1.8 fusion.13
  83.5 1.2 copy.9
  84.7 160.1 %all-gather.3.cloned.1.call-done = bf16[512,8192]{1,0:T(8,128)(2,1)} async-done(((bf16[512,256]{1,0:T(8,128)(2,1)}), bf16[512,8192]{1,0:T(8,128)(2,1)}) %all-gather.3.cloned.1.call-update) | async-done | bytes 8388624 | tf_op jit(solution)/shard_map/all_gather | solution.py:35
  244.8 176.4 %all-gather.5.cloned.1.call-done = bf16[8192,3,256]{0,2,1:T(8,128)(2,1)} async-done(((bf16[512,3,256]{0,2,1:T(8,128)(2,1)}), bf16[8192,3,256]{0,2,1:T(8,128)(2,1)}) %all-gather.5.cloned.1.call-update) | async-done | bytes 12582928 | tf_op jit(solution)/shard_map/all_gather | solution.py:36
  421.1 12.8 %fusion.5 = bf16[512,3,256]{2,0,1:T(8,128)(2,1)S(1)} fusion(bf16[8192,3,256]{0,2,1:T(8,128)(2,1)} %all-gather.5.cloned.1.call-done, bf16[512,8192]{1,0:T(8,128)(2,1)} %all-gather.3.cloned.1.call-done), kind=kOutput, calls=%fused_computation.9 | convolution fusion | flops 6442844160 | bytes 21757952 | tf_op jit(solution)/shard_map/dot_general | solution.py:38
  433.9 1.9 collective-permute-start
  435.9 1.1 collective-permute-done
  437.0 0.2 maximum_convert_fusion
  437.2 0.5 fusion.3
  437.7 0.8 copy.10
  438.5 10.1 %all-to-all-start = ((bf16[16,16,512]{2,1,0:T(8,128)(2,1)}), bf16[16,16,512]{2,1,0:T(8,128)(2,1)S(1)}, u32[]{:S(2)}, u32[]{:S(2)}) async-start(bf16[16,16,512]{2,1,0:T(8,128)(2,1)} %bitcast.10), calls=%async_computation | async-start | bytes 524288 | tf_op jit(solution)/shard_map/all_to_all | solution.py:54
  448.7 96.1 %gather_fusion = bf16[16384]{0:T(1024)(128)(2,1)S(1)} fusion(bf16[128]{0:T(256)(128)(2,1)S(1)} %dynamic-slice_bitcast_fusion, s32[16384]{0:T(1024)S(1)} %fusion.22), kind=kCustom, calls=%fused_computation | custom fusion | bytes 131072 | tf_op jit(solution)/shard_map/gather | solution.py:17
  544.8 0.2 copy.11
  544.9 0.2 reshape.190
  545.1 0.2 reshape.191
  545.3 0.2 fusion.31
  545.5 0.2 fusion.10
  545.7 0.2 convert_element_type.51
  546.1 20.5 %all_to_all.26 = bf16[16,16,512]{2,0,1:T(8,128)(2,1)S(1)} all-to-all(bf16[16,16,512]{2,0,1:T(8,128)(2,1)S(1)} %copy.13), channel_id=1, replica_groups=mesh['ctx'=16,'tp'=32] {'ctx'}, dimensions={1} | all-to-all | bytes 524288 | tf_op jit(solution)/shard_map/all_to_all | solution.py:63
  566.6 0.2 copy.14
  566.8 0.8 fusion.16
  (19 shorter events, 0.4 us)
Async XLA Ops:
  6.5 442.1 %copy-start = (bf16[16,128]{1,0:T(8,128)(2,1)S(1)}, bf16[16,128]{1,0:T(8,128)(2,1)}, u32[]{:S(2)}) copy-start(bf16[16,128]{1,0:T(8,128)(2,1)} %param.9) | copy-start | bytes 12292
  6.5 76.9 %copy-start.1 = (bf16[512,3,256]{2,0,1:T(8,128)(2,1)S(1)}, bf16[512,3,256]{2,0,1:T(8,128)(2,1)}, u32[]{:S(2)}) copy-start(bf16[512,3,256]{2,0,1:T(8,128)(2,1)} %param.7) | copy-start | bytes 2359300
  6.5 238.2 %all-gather.3.cloned.1.call-start = ((), (), s32[]{:S(2)}) async-start(), calls=%async_computation.2 | async-start | bytes 8650752 | tf_op jit(solution)/shard_map/all_gather | solution.py:35
  83.4 337.7 %all-gather.5.cloned.1.call-start = ((), (), s32[]{:S(2)}) async-start(), calls=%async_computation.3 | async-start | bytes 13369344 | tf_op jit(solution)/shard_map/all_gather | solution.py:36
  84.7 351.2 %copy-start.2 = (f32[3,3,256]{2,1,0:T(4,128)S(1)}, f32[3,3,256]{2,1,0:T(4,128)}, u32[]{:S(2)}) copy-start(f32[3,3,256]{2,1,0:T(4,128)} %param.8) | copy-start | bytes 27652
  433.9 3.1 collective-permute-start
  438.5 106.2 %all-to-all-start = ((bf16[16,16,512]{2,1,0:T(8,128)(2,1)}), bf16[16,16,512]{2,1,0:T(8,128)(2,1)S(1)}, u32[]{:S(2)}, u32[]{:S(2)}) async-start(bf16[16,16,512]{2,1,0:T(8,128)(2,1)} %bitcast.10), calls=%async_computation | async-start | bytes 524288 | tf_op jit(solution)/shard_map/all_to_all | solution.py:54
Sparse Core Ops, SparseCore 0:
  83.5 161.1 all-gather.2
  247.9 173.2 all-gather.4
where the time goes:
time: 576 us; the launch traced here: 574 us
  waiting for transfers between devices  338 us (59%)
  local copies, waits for them, and re-layouts  99.1 us (17%)
  blocking collectives  93.7 us (16%)
  between operations  13.6 us (2%)
  matrix products  13.2 us (2%)
  starting transfers between devices  12.1 us (2%)
    all_gather x1, waiting for transfers between devices, per_device(): piece = lax.all_gather(in_weight, 'ctx', axis=0, tiled=True)  176 us
    all_gather x1, waiting for transfers between devices, per_device(): whole = lax.all_gather(normed_local, 'tp', axis=1, tiled=True)  160 us
    gather x1, local copies, waits for them, and re-layouts, toeplitz_pair(): full = rows[:, index]  96.1 us
    psum x1, blocking collectives, per_device(): total_sq = lax.psum(partial_sq, 'tp')  73.2 us
    all_to_all x1, blocking collectives, per_device(): lax.all_to_all(filtered, 'ctx', split_axis=1, concat_axis=0, tiled=True)  20.5 us
    dot_general x1, matrix products, per_device(): jnp.dot(whole, piece.reshape(depth, 3 * local_width), preferred_element_t...  12.8 us
  transfers between devices with their start and end apart: 4, of which 3 were waited for; matrix products, arithmetic and copies ran while one was open for 17% of the time, Pallas kernels for 0%

commit v1 on v0

v1 whole, which is shorter than its diff:
```python
import functools

import jax
import jax.numpy as jnp
from jax import lax
from jax.experimental import pallas as pl
from jax.experimental.pallas import tpu as pltpu
from jax.sharding import PartitionSpec as P

MESH = pl.DeviceIdType.MESH
F32 = jnp.float32
BF16 = jnp.bfloat16
ROWS = 512
COLS = 256
PIECES = 32
TAPS = 128
GROUP = 16
EXT = ROWS + 16
HALO = TAPS + 48


def kernel(
    tok_ref, gain_ref, w_ref, sw_ref, filt_ref, out_ref,
    a_buf, b_buf, xg, stage, acc, sq, toep, proj, gated, qbuf, wide, halo_out, halo_in,
    local_sem, send_sem, a_sem, b_sem, stage_sem, halo_sem,
):
    ctx = lax.axis_index("ctx")
    tp = lax.axis_index("tp")
    core = lax.rem(ctx, 2)
    yh = lax.rem(lax.div(ctx, 2), 2)
    x = lax.div(ctx, 4)
    z = lax.rem(tp, 8)
    yl = lax.div(tp, 8)
    y = yh * 4 + yl

    def at(dx=0, dy=0, dz=0):
        nx, ny, nz = lax.rem(x + dx + 4, 4), lax.rem(y + dy + 8, 8), lax.rem(z + dz + 8, 8)
        return ((nx * 2 + lax.div(ny, 4)) * 2 + core, lax.rem(ny, 4) * 8 + nz)

    lines = [yl, yl + 1 - 2 * lax.rem(yl, 2), lax.rem(yl + 2, 4), 3 - yl]
    line_dev = [(ctx, v * 8 + z) for v in lines]
    up, down = at(dz=1), at(dz=-1)
    east, west = at(dx=1), at(dx=-1)
    sibling = (ctx + 1 - 2 * core, tp)
    after, before = (lax.rem(ctx + 1, 16), tp), (lax.rem(ctx + 15, 16), tp)
    y1, ym1, y3, ym3 = at(dy=1), at(dy=-1), at(dy=3), at(dy=-3)

    sends = []

    def push(src, dst, sem, device):
        copy = pltpu.make_async_remote_copy(
            src_ref=src, dst_ref=dst, send_sem=send_sem.at[len(sends)], recv_sem=sem,
            device_id=device, device_id_type=MESH,
        )
        copy.start()
        sends.append(copy)

    def landed(slot, sem):
        pltpu.make_async_remote_copy(
            src_ref=slot, dst_ref=slot, send_sem=send_sem.at[0], recv_sem=sem,
            device_id=sibling, device_id_type=MESH,
        ).wait_recv()

    own = [
        pltpu.make_async_copy(tok_ref, a_buf.at[tp, pl.ds(0, ROWS)], local_sem.at[0]),
        pltpu.make_async_copy(gain_ref, a_buf.at[tp, pl.ds(ROWS, 16)], local_sem.at[1]),
    ]
    for h in range(2):
        own.append(
            pltpu.make_async_copy(
                w_ref.at[:, pl.ds(h * 256, 256)], b_buf.at[2 * ctx + h], local_sem.at[2 + h]
            )
        )
    for copy in own:
        copy.start()

    barrier = pltpu.get_barrier_semaphore()
    peers = [up, down, east, west, sibling, after, before, y1, ym1, y3, ym3] + line_dev[1:]
    for peer in peers:
        pl.semaphore_signal(barrier, inc=1, device_id=peer, device_id_type=MESH)
    for copy in own:
        copy.wait()
    pl.semaphore_wait(barrier, len(peers))

    def push_a(index, device):
        push(a_buf.at[index], a_buf.at[index], a_sem.at[index], device)

    def push_b(index, device):
        push(b_buf.at[index], b_buf.at[index], b_sem.at[index], device)

    def absorb(t):
        gain = a_buf[t, pl.ds(ROWS, 16), :][0:1].astype(F32)

        @pl.loop(0, ROWS // 64)
        def _(i):
            rows = pl.ds(pl.multiple_of(i * 64, 64), 64)
            values = a_buf[t, rows, :].astype(F32)
            square = values * values
            sq[rows, :] += square[:, :128] + square[:, 128:]
            xg[t, rows, :] = (values * gain).astype(BF16)

    def multiply(t):
        lhs = xg[t]
        for s in range(3):
            acc[s] += jnp.dot(lhs, b_buf[t, s], preferred_element_type=F32)

    mine = [2 * ctx, 2 * ctx + 1]
    push_a(tp, up)
    push_a(tp, down)
    push_b(mine[0], east)
    push_b(mine[1], west)
    push_a(tp, line_dev[1])
    push(b_buf.at[mine[0]], stage.at[0], stage_sem.at[0], y3)
    push(b_buf.at[mine[1]], stage.at[1], stage_sem.at[1], ym3)
    push_b(mine[1], east)
    push_b(mine[0], west)
    push_b(mine[0], sibling)
    push_b(mine[1], sibling)
    push_a(tp, line_dev[2])
    push_a(tp, line_dev[3])

    for s in range(3):
        acc[s] = jnp.zeros((ROWS, COLS), F32)
    sq[...] = jnp.zeros_like(sq)
    tap = lax.broadcasted_iota(jnp.int32, (TAPS, 2 * TAPS), 0)
    place = lax.broadcasted_iota(jnp.int32, (TAPS, 2 * TAPS), 1)
    flip = jnp.where(tap + place == TAPS, 1.0, 0.0).astype(BF16)
    flipped = jnp.dot(filt_ref[...], flip, preferred_element_type=F32)
    for g in range(GROUP):
        row = jnp.broadcast_to(flipped[g : g + 1, :], (TAPS, 2 * TAPS))
        toep[g * TAPS : (g + 1) * TAPS, :] = pltpu.roll(
            row, 0, 1, stride=1, stride_axis=0
        ).astype(BF16)
    absorb(tp)

    events = []
    slot_us, half_us = 5.3, 8.0

    def from_z(r, d, sign, last):
        def act():
            t = lines[r] * 8 + lax.rem(z - sign * d + 8, 8)
            landed(a_buf.at[t], a_sem.at[t])
            if d < last:
                push_a(t, up if sign > 0 else down)
            absorb(t)
        return act

    for sign in (1, -1):
        lasts = [4 if (r % 2 == 0) == (sign > 0) else 3 for r in range(4)]
        first = sorted([(d, r) for r in (0, 1) for d in range(1, lasts[r] + 1)])
        second = sorted([(d, r) for r in (2, 3) for d in range(1, lasts[r] + 1)])
        for k, (d, r) in enumerate(first + second):
            events.append(((k + 1) * slot_us, from_z(r, d, sign, lasts[r])))

    def from_line(r):
        def act():
            t = lines[r] * 8 + z
            landed(a_buf.at[t], a_sem.at[t])
            push_a(t, up)
            push_a(t, down)
            absorb(t)
        return act

    events.append((8.0, from_line(1)))
    events.append((30.0, from_line(2)))
    events.append((32.0, from_line(3)))

    def slot_of(dx, other, h):
        bx = lax.rem(x + dx + 4, 4)
        bh = (1 - yh) if other else yh
        return ((bx * 2 + bh) * 2 + core) * 2 + h

    def from_x(dx, other, h, onward):
        def act():
            t = slot_of(dx, other, h)
            landed(b_buf.at[t], b_sem.at[t])
            if onward is not None:
                push_b(t, onward)
            push_b(t, sibling)
        return act

    for other, base in ((False, 0.0), (True, 3 * half_us)):
        events.append((base + half_us + 0.1, from_x(-1, other, 0, east)))
        events.append((base + half_us + 0.2, from_x(1, other, 1, west)))
        events.append((base + 2 * half_us + 0.1, from_x(-1, other, 1, None)))
        events.append((base + 2 * half_us + 0.2, from_x(1, other, 0, None)))
        events.append((base + 3 * half_us + 0.1, from_x(2, other, 0, None)))
        events.append((base + 3 * half_us + 0.2, from_x(2, other, 1, None)))

    def crossing(h, leg):
        def act():
            if leg == 0:
                landed(stage.at[h], stage_sem.at[h])
                to = y1 if h == 0 else ym1
                origin = lax.rem(y - 3 + 8, 8) if h == 0 else lax.rem(y + 3, 8)
                t = ((x * 2 + lax.div(origin, 4)) * 2 + core) * 2 + h
                push(stage.at[h], b_buf.at[t], b_sem.at[t], to)
            else:
                t = slot_of(0, True, h)
                landed(b_buf.at[t], b_sem.at[t])
                push_b(t, east if h == 0 else west)
                push_b(t, west if h == 0 else east)
                push_b(t, sibling)
        return act

    events.append((15.5, crossing(0, 0)))
    events.append((15.6, crossing(1, 0)))
    events.append((23.0, crossing(0, 1)))
    events.append((23.1, crossing(1, 1)))

    def all_b():
        for k in range(16):
            t = (2 * lax.div(k, 2) + 1 - core) * 2 + (k % 2)
            landed(b_buf.at[t], b_sem.at[t])

        for r in (0, 1):
            @pl.loop(0, 8)
            def _(e):
                multiply(lines[r] * 8 + lax.rem(z + e, 8))

    events.append((56.0, all_b))
    for _, act in sorted(events, key=lambda event: event[0]):
        act()

    for r in (2, 3):
        @pl.loop(0, 8)
        def _(e):
            multiply(lines[r] * 8 + lax.rem(z + e, 8))

    head = proj.at[pl.ds(0, 16)]

    @pl.loop(0, ROWS // 128)
    def _(i):
        rows = pl.ds(pl.multiple_of(i * 128, 128), 128)
        total = jnp.sum(sq[rows, :], axis=1, keepdims=True)
        scale = lax.rsqrt(total / (PIECES * COLS) + 1e-06)
        for s in range(3):
            proj[pl.ds(pl.multiple_of(16 + i * 128, 16), 128), s * COLS : (s + 1) * COLS] = (
                acc[s, rows, :] * scale
            ).astype(BF16)

    def feat(b, s):
        lines_ = pl.ds(pl.multiple_of(b * 128, 16), 144)
        block = proj[lines_, s * COLS : (s + 1) * COLS].astype(F32)
        return (
            sw_ref[0, s : s + 1, :] * block[16:144]
            + sw_ref[1, s : s + 1, :] * block[15:143]
            + sw_ref[2, s : s + 1, :] * block[14:142]
        )

    def gate(b):
        gated[pl.ds(pl.multiple_of((b + 1) * 128, 128), 128), :] = (feat(b, 1) * feat(b, 2)).astype(BF16)

    def mix(b):
        window = gated[pl.ds(pl.multiple_of(b * 128, 128), 256), :]
        lane = lax.broadcasted_iota(jnp.int32, (TAPS, COLS), 1)
        conv = jnp.zeros((TAPS, COLS), F32)
        for g in range(GROUP):
            part = jnp.dot(
                toep[g * TAPS : (g + 1) * TAPS, :], window, preferred_element_type=F32
            )
            inside = (lane >= g * GROUP) & (lane < (g + 1) * GROUP)
            conv = jnp.where(inside, part, conv)
        conv = conv.astype(BF16).astype(F32)
        out_ref[pl.ds(pl.multiple_of(b * 128, 128), 128), :] = (feat(b, 0) * conv).astype(BF16)

    gate(3)
    halo_out[0:TAPS, :] = gated[512:640, :]
    for s in range(3):
        halo_out[TAPS + 16 * s : TAPS + 16 * (s + 1), :] = proj[512:528, s * COLS : (s + 1) * COLS]
    push(halo_out, halo_in, halo_sem.at[0], after)

    gate(1)
    gate(2)
    mix(2)
    mix(3)
    landed(halo_in, halo_sem.at[0])
    keep = jnp.where(ctx > 0, 1.0, 0.0).astype(BF16)
    gated[0:TAPS, :] = halo_in[0:TAPS, :] * keep
    for s in range(3):
        proj[0:16, s * COLS : (s + 1) * COLS] = halo_in[TAPS + 16 * s : TAPS + 16 * (s + 1), :] * keep
    gate(0)
    mix(0)
    mix(1)
    for copy in sends:
        copy.wait_send()


N_SENDS = 80


def per_device(tokens, norm_gain, in_weight, short_weight, filters):
    gains = jnp.broadcast_to(norm_gain[None, :], (16, COLS))
    weight = jnp.transpose(in_weight, (1, 0, 2))
    vmem = pl.BlockSpec(memory_space=pltpu.VMEM)
    hbm = pl.BlockSpec(memory_space=pl.ANY)
    return pl.pallas_call(
        kernel,
        out_shape=jax.ShapeDtypeStruct((ROWS, COLS), BF16),
        in_specs=[hbm, hbm, hbm, vmem, vmem],
        out_specs=vmem,
        scratch_shapes=[
            pltpu.VMEM((PIECES, EXT, COLS), BF16),
            pltpu.VMEM((PIECES, 3, 256, COLS), BF16),
            pltpu.VMEM((PIECES, ROWS, COLS), BF16),
            pltpu.VMEM((2, 3, 256, COLS), BF16),
            pltpu.VMEM((3, ROWS, COLS), F32),
            pltpu.VMEM((ROWS, 128), F32),
            pltpu.VMEM((GROUP * TAPS, 2 * TAPS), BF16),
            pltpu.VMEM((ROWS + 16, 3 * COLS), BF16),
            pltpu.VMEM((ROWS + TAPS, COLS), BF16),
            pltpu.VMEM((16, COLS), BF16),
            pltpu.VMEM((16, COLS), BF16),
            pltpu.VMEM((HALO, COLS), BF16),
            pltpu.VMEM((HALO, COLS), BF16),
            pltpu.SemaphoreType.DMA((4,)),
            pltpu.SemaphoreType.DMA((N_SENDS,)),
            pltpu.SemaphoreType.DMA((PIECES,)),
            pltpu.SemaphoreType.DMA((PIECES,)),
            pltpu.SemaphoreType.DMA((2,)),
            pltpu.SemaphoreType.DMA((1,)),
        ],
        compiler_params=pltpu.CompilerParams(
            collective_id=0, has_side_effects=True, vmem_limit_bytes=58 * 1024 * 1024
        ),
        cost_estimate=pl.CostEstimate(
            flops=2 * ROWS * 8192 * 768, bytes_accessed=4 * 1024 * 1024, transcendentals=0
        ),
    )(tokens, gains, weight, short_weight, filters)


def solution(mesh):
    placed = (P("ctx", "tp"), P("tp"), P("ctx", None, "tp"), P(None, None, "tp"), P("tp", None))
    return jax.shard_map(
        per_device, mesh=mesh, in_specs=placed, out_specs=P("ctx", "tp"), check_vma=False
    )
```

time: 576 us -> 140 us (0.24)
  the two profiles are of different devices: /device:TPU:1 before, /device:TPU:16 now
where the time goes in v1:
time: 140 us
  Pallas kernels  137 us (98%)
  local copies, waits for them, and re-layouts  2.93 us (2%)
    pallas_call x1, Pallas kernels, per_device(): pl.pallas_call(kernel, out_shape=jax.ShapeDtypeStruct((ROWS, COLS), BF16)...  137 us

profile of v1, /device:TPU:16, one launch (start us, length us, event | category | flops | bytes accessed | tf_op | source)
XLA Modules:
  0.0 140.1 jit_solution(7275045848083025388)
XLA Ops:
  0.0 0.0 copy-start
  0.0 0.7 copy-done
  0.7 0.6 broadcast_in_dim.2.gain_ref
  1.3 137.2 %shard_map.55 = bf16[512,256]{1,0:T(8,128)(2,1)} custom-call(bf16[512,256]{1,0:T(8,128)(2,1)} %tok_ref.1, bf16[16,256]{1,0:T(8,128)(2,1)} %broadcast_in_dim.2.gain_ref, bf16[3,512,256]{2,1,0:T(8,128)(2,1)} %bitcast.1, f32[3,3,256]{2,1,0:T(4,128)} %sw_ref.1, bf16[16,128]{1,0:T(8,128)(2,1)} %filt_ref.1), custom_call_target="tpu_custom_call" | custom-call | flops 6442450944 | bytes 4194304 | tf_op jit(solution)/shard_map/pallas_call | solution.py:297
  138.5 1.7 %copy.7 = bf16[512,256]{1,0:T(8,128)(2,1)} copy(bf16[512,256]{1,0:T(8,128)(2,1)} %shard_map.55) | data formatting | bytes 524288
Async XLA Ops:
  0.0 0.7 copy-start

commit v2 on v1

v2 whole, which is shorter than its diff:
```python
import functools

import jax
import jax.numpy as jnp
from jax import lax
from jax.experimental import pallas as pl
from jax.experimental.pallas import tpu as pltpu
from jax.sharding import PartitionSpec as P

MESH = pl.DeviceIdType.MESH
F32 = jnp.float32
BF16 = jnp.bfloat16
ROWS = 512
COLS = 256
PIECES = 32
TAPS = 128
GROUP = 16
EXT = ROWS + 16
HALO = TAPS + 48


def kernel(
    tok_ref, gain_ref, w_ref, sw_ref, filt_ref, out_ref,
    a_buf, b_buf, xg, acc, sq, toep, proj, gated, halo_out, halo_in,
    local_sem, send_sem, a_sem, b_sem, halo_sem,
):
    ctx = lax.axis_index("ctx")
    tp = lax.axis_index("tp")
    core = lax.rem(ctx, 2)
    yh = lax.rem(lax.div(ctx, 2), 2)
    x = lax.div(ctx, 4)
    z = lax.rem(tp, 8)
    yl = lax.div(tp, 8)
    y = yh * 4 + yl

    def at(dx=0, dy=0, dz=0):
        nx, ny, nz = lax.rem(x + dx + 4, 4), lax.rem(y + dy + 8, 8), lax.rem(z + dz + 8, 8)
        return ((nx * 2 + lax.div(ny, 4)) * 2 + core, lax.rem(ny, 4) * 8 + nz)

    lines = [yl, yl + 1 - 2 * lax.rem(yl, 2), lax.rem(yl + 2, 4), 3 - yl]
    line_dev = [(ctx, v * 8 + z) for v in lines]
    up, down = at(dz=1), at(dz=-1)
    east, west = at(dx=1), at(dx=-1)
    sibling = (ctx + 1 - 2 * core, tp)
    after, before = (lax.rem(ctx + 1, 16), tp), (lax.rem(ctx + 15, 16), tp)
    across = at(dy=4)

    sends = []

    def push(src, dst, sem, device):
        copy = pltpu.make_async_remote_copy(
            src_ref=src, dst_ref=dst, send_sem=send_sem.at[len(sends)], recv_sem=sem,
            device_id=device, device_id_type=MESH,
        )
        copy.start()
        sends.append(copy)

    def landed(slot, sem):
        pltpu.make_async_remote_copy(
            src_ref=slot, dst_ref=slot, send_sem=send_sem.at[0], recv_sem=sem,
            device_id=sibling, device_id_type=MESH,
        ).wait_recv()

    own = [
        pltpu.make_async_copy(tok_ref, a_buf.at[tp, pl.ds(0, ROWS)], local_sem.at[0]),
    ]
    for s in range(3):
        columns = pl.ds(s * COLS, COLS)
        own.append(
            pltpu.make_async_copy(w_ref.at[s], b_buf.at[ctx, :, columns], local_sem.at[1 + s])
        )
    for copy in own:
        copy.start()
    a_buf[tp, pl.ds(ROWS, 16), :] = jnp.broadcast_to(gain_ref[...].reshape(1, COLS), (16, COLS))

    barrier = pltpu.get_barrier_semaphore()
    peers = [up, down, east, west, sibling, after, before, across] + line_dev[1:]
    for peer in peers:
        pl.semaphore_signal(barrier, inc=1, device_id=peer, device_id_type=MESH)
    for copy in own:
        copy.wait()
    pl.semaphore_wait(barrier, len(peers))

    def part(t, p):
        rows = pl.ds(0, ROWS // 2) if p == 0 else pl.ds(ROWS // 2, ROWS // 2 + 16)
        return a_buf.at[t, rows], a_sem.at[2 * t + p]

    def push_a(t, p, device):
        ref, sem = part(t, p)
        push(ref, ref, sem, device)

    def half(block, h):
        return b_buf.at[block, pl.ds(h * 256, 256)], b_sem.at[2 * block + h]

    def push_b(block, h, device):
        ref, sem = half(block, h)
        push(ref, ref, sem, device)

    def absorb(t):
        gain = a_buf[t, pl.ds(ROWS, 16), :][0:1].astype(F32)
        columns = pl.ds(pl.multiple_of(lax.rem(t, 2) * COLS, COLS), COLS)

        @pl.loop(0, ROWS // 64)
        def _(i):
            rows = pl.ds(pl.multiple_of(i * 64, 64), 64)
            values = a_buf[t, rows, :].astype(F32)
            square = values * values
            sq[rows, :] += square[:, :128] + square[:, 128:]
            xg[lax.div(t, 2), rows, columns] = (values * gain).astype(BF16)

    def multiply(block):
        @pl.loop(0, ROWS // MUL_ROWS)
        def _(i):
            rows = pl.ds(pl.multiple_of(i * MUL_ROWS, MUL_ROWS), MUL_ROWS)
            acc[rows, :] += jnp.dot(xg[block, rows, :], b_buf[block], preferred_element_type=F32)

    for p in range(2):
        push_a(tp, p, up)
        push_a(tp, p, down)
    push_b(ctx, 0, east)
    push_b(ctx, 1, west)
    for p in range(2):
        push_a(tp, p, line_dev[1])
    push_b(ctx, 1, east)
    push_b(ctx, 0, west)
    push_b(ctx, 0, sibling)
    push_b(ctx, 1, sibling)

    acc[...] = jnp.zeros_like(acc)
    sq[...] = jnp.zeros_like(sq)
    tap = lax.broadcasted_iota(jnp.int32, (TAPS, 2 * TAPS), 0)
    place = lax.broadcasted_iota(jnp.int32, (TAPS, 2 * TAPS), 1)
    flip = jnp.where(tap + place == TAPS, 1.0, 0.0).astype(BF16)
    flipped = jnp.dot(filt_ref[...], flip, preferred_element_type=F32)
    for g in range(GROUP):
        row = jnp.broadcast_to(flipped[g : g + 1, :], (TAPS, 2 * TAPS))
        toep[g * TAPS : (g + 1) * TAPS, :] = pltpu.roll(
            row, 0, 1, stride=1, stride_axis=0
        ).astype(BF16)
    absorb(tp)

    events = []

    def to_line(r):
        def act():
            for p in range(2):
                push_a(tp, p, line_dev[r])
        return act

    for r in (2, 3):
        events.append((LINE_GO_US[r], to_line(r)))

    for h in range(2):
        events.append((CROSS_GO_US[h], functools.partial(push_b, ctx, h, across)))

    halves = set()

    def from_z(r, p, d, sign, last):
        def act():
            t = lines[r] * 8 + lax.rem(z - sign * d + 8, 8)
            landed(*part(t, p))
            if d < last:
                push_a(t, p, up if sign > 0 else down)
            piece = (r, (-sign * d) % 8)
            if piece in halves:
                absorb(t)
            halves.add(piece)
        return act

    for sign in (1, -1):
        for at_us, r, p, d, last in ring_times(sign):
            events.append((at_us, from_z(r, p, d, sign, last)))

    def from_line(r):
        def act():
            t = lines[r] * 8 + z
            for p in range(2):
                landed(*part(t, p))
                push_a(t, p, up)
                push_a(t, p, down)
            absorb(t)
        return act

    for r in (1, 2, 3):
        events.append((LINE_US[r], from_line(r)))

    half_us = 8.4

    def from_x(dx, other, h, onward):
        def act():
            bx = lax.rem(x + dx + 4, 4)
            bh = (1 - yh) if other else yh
            block = (bx * 2 + bh) * 2 + core
            landed(*half(block, h))
            for device in onward:
                push_b(block, h, device)
            push_b(block, h, sibling)
        return act

    for other in (False, True):
        base0, base1 = CROSS_US if other else (0.0, 0.0)
        if other:
            events.append((base0, from_x(0, other, 0, (east, west))))
            events.append((base1, from_x(0, other, 1, (west, east))))
        events.append((base0 + half_us + 0.1, from_x(-1, other, 0, (east,))))
        events.append((base1 + half_us + 0.2, from_x(1, other, 1, (west,))))
        late0, late1 = (1, 1) if other else (2, 2)
        events.append((base1 + late1 * half_us + 0.3, from_x(-1, other, 1, ())))
        events.append((base0 + late0 * half_us + 0.4, from_x(1, other, 0, ())))
        far0, far1 = (2, 2) if other else (3, 3)
        events.append((base0 + far0 * half_us + 0.5, from_x(2, other, 0, ())))
        events.append((base1 + far1 * half_us + 0.5, from_x(2, other, 1, ())))

    def near_products(r, other_core):
        def act():
            block = (lines[r] * 2 + yh) * 2 + (1 - core if other_core else core)
            if other_core:
                for h in range(2):
                    landed(*half(block, h))
            multiply(block)
        return act

    for r in range(NEAR):
        for k, other_core in enumerate((False, True)):
            ready = max(t for sign in (1, -1) for t, q, *_ in ring_times(sign) if q == r)
            events.append((max(ready + 0.1, 33.0) + 2 * k, near_products(r, other_core)))

    def all_b(r):
        def act():
            for bh in (yh, 1 - yh) if r >= NEAR else (1 - yh,):
                block = (lines[r] * 2 + bh) * 2 + 1 - core
                for h in range(2):
                    landed(*half(block, h))
        return act

    def far_products(r, cc):
        def act():
            multiply((lines[r] * 2 + 1 - yh) * 2 + cc)
        return act

    def products(r, j):
        def act():
            multiply(lines[r] * 4 + lax.rem(lax.div(z, 2) + j, 4))
        return act

    three_hops = max(t for sign in (1, -1) for t, r, p, d, last in ring_times(sign) if d < 4)
    for r in range(4):
        events.append((ALL_B_US, all_b(r)))
    for r in range(NEAR):
        for cc in range(2):
            events.append((ALL_B_US + 0.9 * (2 * r + cc + 1), far_products(r, cc)))
    for r in range(NEAR, 4):
        events.append((ALL_B_US + 6, products(r, 0)))
        for j in (1, 3):
            assert ALL_B_US + 0.9 * 2 * NEAR < three_hops
            events.append((max(ALL_B_US + 6, three_hops + 0.1) + 0.01 * j, products(r, j)))
        events.append((200.0, products(r, 2)))
    for _, act in sorted(events, key=lambda event: event[0]):
        act()

    @pl.loop(0, ROWS // 128)
    def _(i):
        rows = pl.ds(pl.multiple_of(i * 128, 128), 128)
        total = jnp.sum(sq[rows, :], axis=1, keepdims=True)
        scale = lax.rsqrt(total / (PIECES * COLS) + 1e-06)
        for s in range(3):
            proj[pl.ds(pl.multiple_of(16 + i * 128, 16), 128), s * COLS : (s + 1) * COLS] = (
                acc[rows, s * COLS : (s + 1) * COLS] * scale
            ).astype(BF16)

    def feat(b, s):
        lines_ = pl.ds(pl.multiple_of(b * 128, 16), 144)
        block = proj[lines_, s * COLS : (s + 1) * COLS].astype(F32)
        return (
            sw_ref[0, s : s + 1, :] * block[16:144]
            + sw_ref[1, s : s + 1, :] * block[15:143]
            + sw_ref[2, s : s + 1, :] * block[14:142]
        )

    def gate(b):
        gated[pl.ds(pl.multiple_of((b + 1) * 128, 128), 128), :] = (feat(b, 1) * feat(b, 2)).astype(BF16)

    def mix(b):
        window = gated[pl.ds(pl.multiple_of(b * 128, 128), 256), :]
        lane = lax.broadcasted_iota(jnp.int32, (TAPS, COLS), 1)
        conv = jnp.zeros((TAPS, COLS), F32)
        for g in range(GROUP):
            part = jnp.dot(
                toep[g * TAPS : (g + 1) * TAPS, :], window, preferred_element_type=F32
            )
            inside = (lane >= g * GROUP) & (lane < (g + 1) * GROUP)
            conv = jnp.where(inside, part, conv)
        conv = conv.astype(BF16).astype(F32)
        out_ref[pl.ds(pl.multiple_of(b * 128, 128), 128), :] = (feat(b, 0) * conv).astype(BF16)

    gate(3)
    halo_out[0:TAPS, :] = gated[512:640, :]
    for s in range(3):
        halo_out[TAPS + 16 * s : TAPS + 16 * (s + 1), :] = proj[512:528, s * COLS : (s + 1) * COLS]
    push(halo_out, halo_in, halo_sem.at[0], after)

    gate(1)
    gate(2)
    mix(2)
    mix(3)
    landed(halo_in, halo_sem.at[0])
    keep = jnp.where(ctx > 0, 1.0, 0.0).astype(BF16)
    gated[0:TAPS, :] = halo_in[0:TAPS, :] * keep
    for s in range(3):
        proj[0:16, s * COLS : (s + 1) * COLS] = halo_in[TAPS + 16 * s : TAPS + 16 * (s + 1), :] * keep
    gate(0)
    mix(0)
    mix(1)
    for copy in sends:
        copy.wait_send()


N_SENDS = 120
MUL_ROWS = 256
NEAR = 3
LINE_GO_US = (0.0, 0.0, 0.1, 0.2)
LINE_US = (0.0, 12.0, 36.0, 58.0)
CROSS_GO_US = (24.0, 24.1)
CROSS_US = (54.0, 59.0)
ALL_B_US = 81.0


def ring_times(sign):
    part_us, delay_us = 3.2, 1.0
    waiting = []
    for r in range(4):
        for p in range(2):
            waiting.append((max(LINE_US[r], 0.0), r, p, 1))
    free, times = 0.0, []
    while waiting:
        waiting.sort()
        ready, r, p, d = waiting.pop(0)
        free = max(free, ready) + part_us
        last = 4 if (p == 0) == (sign > 0) else 3
        times.append((free + delay_us + (0.01 if sign < 0 else 0.0), r, p, d, last))
        if d < last:
            waiting.append((free + delay_us, r, p, d + 1))
    return times


def per_device(tokens, norm_gain, in_weight, short_weight, filters):
    weight = jnp.transpose(in_weight, (1, 0, 2))
    vmem = pl.BlockSpec(memory_space=pltpu.VMEM)
    hbm = pl.BlockSpec(memory_space=pl.ANY)
    return pl.pallas_call(
        kernel,
        out_shape=jax.ShapeDtypeStruct((ROWS, COLS), BF16),
        in_specs=[hbm, vmem, hbm, vmem, vmem],
        out_specs=vmem,
        scratch_shapes=[
            pltpu.VMEM((PIECES, EXT, COLS), BF16),
            pltpu.VMEM((PIECES // 2, 2 * COLS, 3 * COLS), BF16),
            pltpu.VMEM((PIECES // 2, ROWS, 2 * COLS), BF16),
            pltpu.VMEM((ROWS, 3 * COLS), F32),
            pltpu.VMEM((ROWS, 128), F32),
            pltpu.VMEM((GROUP * TAPS, 2 * TAPS), BF16),
            pltpu.VMEM((ROWS + 16, 3 * COLS), BF16),
            pltpu.VMEM((ROWS + TAPS, COLS), BF16),
            pltpu.VMEM((HALO, COLS), BF16),
            pltpu.VMEM((HALO, COLS), BF16),
            pltpu.SemaphoreType.DMA((4,)),
            pltpu.SemaphoreType.DMA((N_SENDS,)),
            pltpu.SemaphoreType.DMA((2 * PIECES,)),
            pltpu.SemaphoreType.DMA((PIECES,)),
            pltpu.SemaphoreType.DMA((1,)),
        ],
        compiler_params=pltpu.CompilerParams(
            collective_id=0, has_side_effects=True, vmem_limit_bytes=58 * 1024 * 1024
        ),
        cost_estimate=pl.CostEstimate(
            flops=2 * ROWS * 8192 * 768, bytes_accessed=4 * 1024 * 1024, transcendentals=0
        ),
    )(tokens, norm_gain, weight, short_weight, filters)


def solution(mesh):
    placed = (P("ctx", "tp"), P("tp"), P("ctx", None, "tp"), P(None, None, "tp"), P("tp", None))
    return jax.shard_map(
        per_device, mesh=mesh, in_specs=placed, out_specs=P("ctx", "tp"), check_vma=False
    )
```

time: 140 us -> 117 us (0.84)
  the two profiles are of different devices: /device:TPU:16 before, /device:TPU:1 now
where the time goes in v2:
time: 117 us; the launch traced here: 115 us
  Pallas kernels  114 us (97%)
  local copies, waits for them, and re-layouts  1.67 us (1%)
    pallas_call x1, Pallas kernels, per_device(): pl.pallas_call(kernel, out_shape=jax.ShapeDtypeStruct((ROWS, COLS), BF16)...  114 us

profile of v2, /device:TPU:1, one launch (start us, length us, event | category | flops | bytes accessed | tf_op | source)
XLA Modules:
  0.0 115.4 jit_solution(9830396682459834203)
XLA Ops:
  0.0 113.7 %shard_map.55 = bf16[512,256]{1,0:T(8,128)(2,1)} custom-call(bf16[512,256]{1,0:T(8,128)(2,1)} %tok_ref.1, bf16[256]{0:T(256)(128)(2,1)} %gain_ref.1, bf16[3,512,256]{2,1,0:T(8,128)(2,1)} %bitcast.1, f32[3,3,256]{2,1,0:T(4,128)} %sw_ref.1, bf16[16,128]{1,0:T(8,128)(2,1)} %filt_ref.1), custom_call_target="tpu_custom_call" | custom-call | flops 6442450944 | bytes 4194304 | tf_op jit(solution)/shard_map/pallas_call | solution.py:350
  113.7 1.7 %copy.7 = bf16[512,256]{1,0:T(8,128)(2,1)} copy(bf16[512,256]{1,0:T(8,128)(2,1)} %shard_map.55) | data formatting | bytes 524288

commit v3 on v2

--- a/solution.py
+++ b/solution.py
@@ -248,12 +248,11 @@
         events.append((ALL_B_US, all_b(r)))
     for r in range(NEAR):
         for cc in range(2):
-            events.append((ALL_B_US + 0.9 * (2 * r + cc + 1), far_products(r, cc)))
+            events.append((ALL_B_US + 0.4 * (2 * r + cc + 1), far_products(r, cc)))
     for r in range(NEAR, 4):
-        events.append((ALL_B_US + 6, products(r, 0)))
+        events.append((ALL_B_US + 2.6, products(r, 0)))
         for j in (1, 3):
-            assert ALL_B_US + 0.9 * 2 * NEAR < three_hops
-            events.append((max(ALL_B_US + 6, three_hops + 0.1) + 0.01 * j, products(r, j)))
+            events.append((max(ALL_B_US + 2.7, three_hops + 0.1) + 0.01 * j, products(r, j)))
         events.append((200.0, products(r, 2)))
     for _, act in sorted(events, key=lambda event: event[0]):
         act()
@@ -321,8 +320,8 @@
 LINE_GO_US = (0.0, 0.0, 0.1, 0.2)
 LINE_US = (0.0, 12.0, 36.0, 58.0)
 CROSS_GO_US = (24.0, 24.1)
-CROSS_US = (54.0, 59.0)
-ALL_B_US = 81.0
+CROSS_US = (50.0, 52.0)
+ALL_B_US = 84.6
 
 
 def ring_times(sign):

time: 117 us -> 120 us (1.026)
  Pallas kernels: 114 us -> 118 us
    pallas_call x1, Pallas kernels: 114 us -> 118 us  [per_device(): pl.pallas_call(kernel, out_shape=jax.ShapeDtypeStruct((ROWS, COLS), BF16)...]
where the time goes in v3:
time: 120 us; the launch traced here: 119 us
  Pallas kernels  118 us (98%)
  local copies, waits for them, and re-layouts  1.67 us (1%)
    pallas_call x1, Pallas kernels, per_device(): pl.pallas_call(kernel, out_shape=jax.ShapeDtypeStruct((ROWS, COLS), BF16)...  118 us

profile of v3, /device:TPU:1, one launch (start us, length us, event | category | flops | bytes accessed | tf_op | source)
XLA Modules:
  0.0 119.4 jit_solution(9605773755543009755)
XLA Ops:
  0.0 117.7 %shard_map.55 = bf16[512,256]{1,0:T(8,128)(2,1)} custom-call(bf16[512,256]{1,0:T(8,128)(2,1)} %tok_ref.1, bf16[256]{0:T(256)(128)(2,1)} %gain_ref.1, bf16[3,512,256]{2,1,0:T(8,128)(2,1)} %bitcast.1, f32[3,3,256]{2,1,0:T(4,128)} %sw_ref.1, bf16[16,128]{1,0:T(8,128)(2,1)} %filt_ref.1), custom_call_target="tpu_custom_call" | custom-call | flops 6442450944 | bytes 4194304 | tf_op jit(solution)/shard_map/pallas_call | solution.py:349
  117.7 1.7 %copy.7 = bf16[512,256]{1,0:T(8,128)(2,1)} copy(bf16[512,256]{1,0:T(8,128)(2,1)} %shard_map.55) | data formatting | bytes 524288

commit v4 on v3

--- a/solution.py
+++ b/solution.py
@@ -320,7 +320,7 @@
 LINE_GO_US = (0.0, 0.0, 0.1, 0.2)
 LINE_US = (0.0, 12.0, 36.0, 58.0)
 CROSS_GO_US = (24.0, 24.1)
-CROSS_US = (50.0, 52.0)
+CROSS_US = (56.0, 58.5)
 ALL_B_US = 84.6
 
 

time: 120 us -> 118 us (0.983)
  Pallas kernels: 118 us -> 116 us
    pallas_call x1, Pallas kernels: 118 us -> 116 us  [per_device(): pl.pallas_call(kernel, out_shape=jax.ShapeDtypeStruct((ROWS, COLS), BF16)...]
where the time goes in v4:
time: 118 us
  Pallas kernels  116 us (98%)
  local copies, waits for them, and re-layouts  1.67 us (1%)
    pallas_call x1, Pallas kernels, per_device(): pl.pallas_call(kernel, out_shape=jax.ShapeDtypeStruct((ROWS, COLS), BF16)...  116 us

profile of v4, /device:TPU:1, one launch (start us, length us, event | category | flops | bytes accessed | tf_op | source)
XLA Modules:
  0.0 117.6 jit_solution(11200571543305027963)
XLA Ops:
  0.0 116.0 %shard_map.55 = bf16[512,256]{1,0:T(8,128)(2,1)} custom-call(bf16[512,256]{1,0:T(8,128)(2,1)} %tok_ref.1, bf16[256]{0:T(256)(128)(2,1)} %gain_ref.1, bf16[3,512,256]{2,1,0:T(8,128)(2,1)} %bitcast.1, f32[3,3,256]{2,1,0:T(4,128)} %sw_ref.1, bf16[16,128]{1,0:T(8,128)(2,1)} %filt_ref.1), custom_call_target="tpu_custom_call" | custom-call | flops 6442450944 | bytes 4194304 | tf_op jit(solution)/shard_map/pallas_call | solution.py:349
  116.0 1.7 %copy.7 = bf16[512,256]{1,0:T(8,128)(2,1)} copy(bf16[512,256]{1,0:T(8,128)(2,1)} %shard_map.55) | data formatting | bytes 524288

commit v5 on v4

--- a/solution.py
+++ b/solution.py
@@ -317,10 +317,10 @@
 N_SENDS = 120
 MUL_ROWS = 256
 NEAR = 3
-LINE_GO_US = (0.0, 0.0, 0.1, 0.2)
+LINE_GO_US = (0.0, 0.0, 0.1, 32.0)
 LINE_US = (0.0, 12.0, 36.0, 58.0)
-CROSS_GO_US = (24.0, 24.1)
-CROSS_US = (56.0, 58.5)
+CROSS_GO_US = (15.0, 15.1)
+CROSS_US = (50.0, 54.0)
 ALL_B_US = 84.6
 
 

time: 118 us -> 116 us (0.983)
  Pallas kernels: 116 us -> 113 us
    pallas_call x1, Pallas kernels: 116 us -> 113 us  [per_device(): pl.pallas_call(kernel, out_shape=jax.ShapeDtypeStruct((ROWS, COLS), BF16)...]
where the time goes in v5:
time: 116 us; the launch traced here: 115 us
  Pallas kernels  113 us (97%)
  local copies, waits for them, and re-layouts  1.67 us (1%)
    pallas_call x1, Pallas kernels, per_device(): pl.pallas_call(kernel, out_shape=jax.ShapeDtypeStruct((ROWS, COLS), BF16)...  113 us

profile of v5, /device:TPU:1, one launch (start us, length us, event | category | flops | bytes accessed | tf_op | source)
XLA Modules:
  0.0 115.0 jit_solution(2405887551120449130)
XLA Ops:
  0.0 113.4 %shard_map.55 = bf16[512,256]{1,0:T(8,128)(2,1)} custom-call(bf16[512,256]{1,0:T(8,128)(2,1)} %tok_ref.1, bf16[256]{0:T(256)(128)(2,1)} %gain_ref.1, bf16[3,512,256]{2,1,0:T(8,128)(2,1)} %bitcast.1, f32[3,3,256]{2,1,0:T(4,128)} %sw_ref.1, bf16[16,128]{1,0:T(8,128)(2,1)} %filt_ref.1), custom_call_target="tpu_custom_call" | custom-call | flops 6442450944 | bytes 4194304 | tf_op jit(solution)/shard_map/pallas_call | solution.py:349
  113.4 1.7 %copy.7 = bf16[512,256]{1,0:T(8,128)(2,1)} copy(bf16[512,256]{1,0:T(8,128)(2,1)} %shard_map.55) | data formatting | bytes 524288
